TPU v7x, 512 devices: a whole 4x4x16 slice. The times are simulated.
512 devices in a mesh: day: 64 (over z, y), pair: 8 (over x, core).
Axes of the slice: x: 4, y: 4, z: 16, core: 2. Of those that a mesh axis runs over, the one named last changes fastest.
Arguments:
- spectra: bfloat16 [128, 128, 4096], P('day', 'pair'), may hold values from -40 to 40
- pair_stations: int32 [512, 2], P('pair'), may hold values from 0 to 127
- availability: int32 [128, 128], P('day'), may hold values from 0 to 1
Outputs:
- stacks: bfloat16 [128, 512, 1001], P('day', 'pair')
- reference: float32 [512, 1001], P('pair')
All inputs are finite; a program needn't handle non-finite values.
Results may differ from a plain program's by a relative error of at most 0.008.
Values may be sent and summed in bfloat16 or wider, within the bound.
A program may use at most 64 MiB of HBM per device.

v0:
```python
import jax
import jax.numpy as jnp
import numpy as np
from jax import lax
from jax.sharding import PartitionSpec as P

LAGS = 1001
WIDE = 1024
WINDOW = 30


def lag_table(bin_count):
    bin_ids = np.arange(bin_count)[:, None]
    lag_ids = np.arange(LAGS)[None, :] - (LAGS - 1) // 2
    angle = np.mod(bin_ids * lag_ids, 2 * bin_count) * (np.pi / bin_count)
    factor = 1.0 / np.sqrt(2.0 * bin_count)
    table = np.concatenate([np.cos(angle) * factor, -np.sin(angle) * factor], 0)
    return np.pad(table, ((0, 0), (0, WIDE - LAGS))).astype(np.float32).astype(jnp.bfloat16)


def per_device(spectra, pair_stations, availability):
    days_here = spectra.shape[0]
    groups = lax.axis_size("day")
    station_count = spectra.shape[1] * lax.axis_size("pair")
    bin_count = spectra.shape[2] // 2
    pairs_here = pair_stations.shape[0]
    inverse = jnp.asarray(lag_table(bin_count))
    station_ids = jnp.arange(station_count, dtype=jnp.int32)
    ends = jnp.concatenate([pair_stations[:, 0], pair_stations[:, 1]], 0)
    pick = (ends[:, None] == station_ids[None, :]).astype(jnp.bfloat16)
    avail = jnp.dot(availability.astype(jnp.bfloat16), pick.T, preferred_element_type=jnp.float32)
    present = avail[:, :pairs_here] * avail[:, pairs_here:]
    gathered = lax.all_gather(spectra, "pair", axis=1, tiled=True)
    rows = []
    for day in range(days_here):
        spec = jnp.dot(pick, gathered[day], preferred_element_type=jnp.float32)
        one, two = (spec[:pairs_here], spec[pairs_here:])
        ar, ai, br, bi = (
            one[:, :bin_count],
            one[:, bin_count:],
            two[:, :bin_count],
            two[:, bin_count:],
        )
        rows.append(jnp.concatenate([ar * br + ai * bi, ar * bi - ai * br], 1).astype(jnp.bfloat16))
    cross = jnp.concatenate(rows, 0)
    corr = jnp.dot(cross, inverse, preferred_element_type=jnp.float32)
    column = lax.broadcasted_iota(jnp.int32, (1, WIDE), 1)
    shown = present.reshape(-1, 1)
    daily = jnp.where(column == LAGS, shown, corr * shown).astype(jnp.bfloat16)
    daily = daily.reshape(days_here, pairs_here, WIDE)
    turned = lax.all_to_all(daily, "day", split_axis=1, concat_axis=0, tiled=True)
    days = groups * days_here
    mine = turned.reshape(days, WIDE)
    day_ids = np.arange(days)
    gap = day_ids[:, None] - day_ids[None, :]
    band = jnp.asarray(((gap >= 0) & (gap < WINDOW)).astype(np.float32), dtype=jnp.bfloat16)
    moving = jnp.dot(band, mine, preferred_element_type=jnp.float32)
    counts = moving[:, LAGS : LAGS + 1]
    ref = jnp.sum(mine.astype(jnp.float32), axis=0) / days
    ref = jnp.where(column[0] < LAGS, ref, 0.0)
    scale = jnp.sqrt(jnp.sum(ref * ref) / LAGS + 1e-06)
    stacks = (moving / jnp.maximum(counts, 1.0) / scale).astype(jnp.bfloat16)
    back = lax.all_to_all(
        stacks.reshape(days, 1, WIDE), "day", split_axis=0, concat_axis=1, tiled=True
    )
    ref_all = lax.all_gather(ref[None], "day", axis=0, tiled=True)
    return (back[:, :, :LAGS], ref_all[:, :LAGS])


def solution(mesh):
    return jax.shard_map(
        per_device,
        mesh=mesh,
        in_specs=(P("day", "pair", None), P("pair", None), P("day", None)),
        out_specs=(P("day", "pair", None), P("pair", None)),
        check_vma=False,
    )
```

profile of v0, /device:TPU:8, one launch (start us, length us, event | category | flops | bytes accessed | tf_op | source)
XLA Modules:
  0.0 198.5 jit_solution(13838983268094882941)
XLA Ops:
  7.2 0.0 all-gather.3.cloned.1.call-start
  7.2 0.7 all-gather.3.cloned.1.call-update
  7.9 0.8 slice_bitcast_fusion.5
  8.7 0.1 pad_add_fusion
  8.7 0.9 convolution_bitcast_fusion
  9.6 0.1 slice_multiply_fusion
  9.7 0.1 broadcast_in_dim.28
  9.8 37.6 %all-gather.3.cloned.1.call-done = bf16[2,128,4096]{2,1,0:T(8,128)(2,1)} async-done(((bf16[2,16,4096]{2,1,0:T(8,128)(2,1)}), bf16[2,128,4096]{2,1,0:T(8,128)(2,1)}) %all-gather.3.cloned.1.call-update) | async-done | bytes 2097168 | tf_op jit(solution)/shard_map/all_gather | solution.py:33
  47.4 0.0 copy-start
  47.4 1.8 fusion.3
  49.2 0.1 copy-done
  49.3 0.0 copy-start.2
  49.3 0.5 fusion.2
  49.8 0.4 add_convert_fusion
  50.2 2.5 %copy-done.2 = bf16[4096,1024]{1,0:T(8,128)(2,1)S(1)} copy-done((bf16[4096,1024]{1,0:T(8,128)(2,1)S(1)}, bf16[4096,1024]{1,0:T(8,128)(2,1)}, u32[]{:S(2)}) %copy-start.2) | copy-done | bytes 8388632
  52.7 0.0 copy-start.1
  52.7 1.3 fusion.1
  54.0 0.3 copy.12
  54.3 37.4 %all_to_all.33 = bf16[2,64,1024]{2,0,1:T(2,128)(2,1)S(1)} all-to-all(bf16[2,64,1024]{2,0,1:T(2,128)(2,1)S(1)} %copy.12), channel_id=1, replica_groups=mesh['day'=64,'pair'=8] {'day'}, dimensions={1} | all-to-all | bytes 524288 | tf_op jit(solution)/shard_map/all_to_all | solution.py:51
  91.7 0.2 convert_reduce_fusion
  91.9 0.6 broadcast_multiply_fusion
  93.3 0.0 copy-done.1
  93.3 0.2 fusion.18
  93.5 0.2 fusion.11
  93.7 0.1 fusion.9
  93.8 0.5 broadcast.36
  94.3 0.8 reduce.6
  95.1 0.8 reshape.58
  95.9 5.9 %all-to-all-start.1 = ((bf16[64,2,1024]{2,1,0:T(2,128)(2,1)}), bf16[64,2,1024]{2,1,0:T(2,128)(2,1)S(1)}, u32[]{:S(2)}, u32[]{:S(2)}) async-start(bf16[64,2,1024]{2,1,0:T(2,128)(2,1)} %reshape.58), calls=%async_computation.1 | async-start | bytes 524288 | tf_op jit(solution)/shard_map/all_to_all | solution.py:63
  101.9 86.4 %all-gather = f32[64,1,1024]{2,1,0:T(1,128)S(1)} all-gather(f32[1,1,1024]{2,1,0:T(1,128)S(1)} %fusion.15), channel_id=1, replica_groups=mesh['day'=64,'pair'=8] {'day'}, dimensions={0}, use_global_device_ids=true | all-gather | bytes 266240 | tf_op jit(solution)/shard_map/all_gather | solution.py:66
  188.3 0.8 copy.19
  189.1 0.0 all-to-all-done.1
  189.1 0.2 reshape.59
  189.3 1.5 reduce.4
  190.8 0.1 all_to_all.28
  190.9 0.8 copy.15
  (3 shorter events, 0.1 us)
Async XLA Ops:
  7.2 40.2 %all-gather.3.cloned.1.call-start = ((), (), s32[]{:S(2)}) async-start(), calls=%async_computation.2 | async-start | bytes 2359296 | tf_op jit(solution)/shard_map/all_gather | solution.py:33
  47.4 1.9 copy-start
  49.3 3.4 %copy-start.2 = (bf16[4096,1024]{1,0:T(8,128)(2,1)S(1)}, bf16[4096,1024]{1,0:T(8,128)(2,1)}, u32[]{:S(2)}) copy-start(bf16[4096,1024]{1,0:T(8,128)(2,1)} %constant.19.clone) | copy-start | bytes 25165828
  52.7 40.6 %copy-start.1 = (bf16[128,128]{1,0:T(8,128)(2,1)S(1)}, bf16[128,128]{1,0:T(8,128)(2,1)}, u32[]{:S(2)}) copy-start(bf16[128,128]{1,0:T(8,128)(2,1)} %constant.25) | copy-start | bytes 98308
  95.9 93.1 %all-to-all-start.1 = ((bf16[64,2,1024]{2,1,0:T(2,128)(2,1)}), bf16[64,2,1024]{2,1,0:T(2,128)(2,1)S(1)}, u32[]{:S(2)}, u32[]{:S(2)}) async-start(bf16[64,2,1024]{2,1,0:T(2,128)(2,1)} %reshape.58), calls=%async_computation.1 | async-start | bytes 524288 | tf_op jit(solution)/shard_map/all_to_all | solution.py:63
Sparse Core Ops, SparseCore 0:
  10.1 37.1 all-gather.2
where the time goes:
time: 199 us
  blocking collectives  124 us (62%)
  waiting for transfers between devices  38.3 us (19%)
  between operations  14.8 us (7%)
  local copies, waits for them, and re-layouts  6.83 us (3%)
  starting transfers between devices  5.97 us (3%)
  matrix products  4.73 us (2%)
  other arithmetic  4.04 us (2%)
    all_gather x1, blocking collectives, per_device(): ref_all = lax.all_gather(ref[None], 'day', axis=0, tiled=True)  86.4 us
    all_gather x1, waiting for transfers between devices, per_device(): gathered = lax.all_gather(spectra, 'pair', axis=1, tiled=True)  37.6 us
    all_to_all x1, blocking collectives, per_device(): lax.all_to_all(daily, 'day', split_axis=1, concat_axis=0, tiled=True)  37.4 us
    all_to_all x1, starting transfers between devices, per_device(): lax.all_to_all(stacks.reshape(days, 1, WIDE), 'day', split_axis=0, concat...  5.93 us
    unnamed x10, local copies, waits for them, and re-layouts  5.05 us
  transfers between devices with their start and end apart: 2, of which 1 were waited for; matrix products, arithmetic and copies ran while one was open for 1% of the time, Pallas kernels for 0%

commit v1 on v0

--- a/solution.py
+++ b/solution.py
@@ -30,7 +30,12 @@
     pick = (ends[:, None] == station_ids[None, :]).astype(jnp.bfloat16)
     avail = jnp.dot(availability.astype(jnp.bfloat16), pick.T, preferred_element_type=jnp.float32)
     present = avail[:, :pairs_here] * avail[:, pairs_here:]
-    gathered = lax.all_gather(spectra, "pair", axis=1, tiled=True)
+    ring = [spectra]
+    for hop in range(7):
+        ring.append(lax.ppermute(ring[-1], "pair", [(dev, (dev + 1) % 8) for dev in range(8)]))
+    gathered = jnp.roll(
+        jnp.concatenate(ring[::-1], axis=1), (lax.axis_index("pair") + 1) * ring[0].shape[1], axis=1
+    )
     rows = []
     for day in range(days_here):
         spec = jnp.dot(pick, gathered[day], preferred_element_type=jnp.float32)

time: 199 us -> 189 us (0.950)
  between operations: 14.8 us -> 1.61 us
  waiting for transfers between devices: 38.3 us -> 47.4 us
  blocking collectives: 124 us -> 119 us
    ppermute x0 -> x7, waiting for transfers between devices: none -> 47.4 us  [per_device(): lax.ppermute(ring[-1], 'pair', [(dev, (dev + 1) % 8) for dev in range(8)])]
    all_gather x1 -> x0, waiting for transfers between devices: 37.6 us -> none  [per_device(): gathered = lax.all_gather(spectra, 'pair', axis=1, tiled=True)]
    all_gather x1, blocking collectives: 86.4 us -> 82.9 us  [per_device(): ref_all = lax.all_gather(ref[None], 'day', axis=0, tiled=True)]
    unnamed x10 -> x27, local copies, waits for them, and re-layouts: 5.05 us -> 5.78 us
  transfers between devices with their start and end apart: 2 -> 8, of which waited for: 1 -> 7; matrix products, arithmetic and copies ran while one was open for 1% -> 1% of each run, Pallas kernels for 0% -> 0%
where the time goes in v1:
time: 189 us
  blocking collectives  119 us (63%)
  waiting for transfers between devices  47.4 us (25%)
  local copies, waits for them, and re-layouts  7.58 us (4%)
  starting transfers between devices  5.75 us (3%)
  other arithmetic  4.03 us (2%)
  matrix products  3.36 us (2%)
    all_gather x1, blocking collectives, per_device(): ref_all = lax.all_gather(ref[None], 'day', axis=0, tiled=True)  82.9 us
    ppermute x7, waiting for transfers between devices, per_device(): lax.ppermute(ring[-1], 'pair', [(dev, (dev + 1) % 8) for dev in range(8)])  47.4 us
    all_to_all x1, blocking collectives, per_device(): lax.all_to_all(daily, 'day', split_axis=1, concat_axis=0, tiled=True)  36 us
    unnamed x27, local copies, waits for them, and re-layouts  5.78 us
    all_to_all x1, starting transfers between devices, per_device(): lax.all_to_all(stacks.reshape(days, 1, WIDE), 'day', split_axis=0, concat...  5.71 us
  transfers between devices with their start and end apart: 8, of which 7 were waited for; matrix products, arithmetic and copies ran while one was open for 1% of the time, Pallas kernels for 0%

profile of v1, /device:TPU:8, one launch (start us, length us, event | category | flops | bytes accessed | tf_op | source)
XLA Modules:
  0.0 188.6 jit_solution(9228744218664644967)
XLA Ops:
  0.6 0.0 copy-start
  0.6 0.0 collective-permute-start
  0.7 7.2 %collective-permute-done = bf16[2,16,4096]{2,1,0:T(8,128)(2,1)S(1)} collective-permute-done((bf16[2,16,4096]{2,1,0:T(8,128)(2,1)}, bf16[2,16,4096]{2,1,0:T(8,128)(2,1)S(1)}, u32[]{:S(2)}, u32[]{:S(2)}) %collective-permute-start) | collective-permute-done | bytes 262176 | tf_op jit(solution)/shard_map/ppermute | solution.py:35
  7.9 0.0 collective-permute-start.1
  7.9 7.0 %collective-permute-done.1 = bf16[2,16,4096]{2,1,0:T(8,128)(2,1)S(1)} collective-permute-done((bf16[2,16,4096]{2,1,0:T(8,128)(2,1)S(1)}, bf16[2,16,4096]{2,1,0:T(8,128)(2,1)S(1)}, u32[]{:S(2)}, u32[]{:S(2)}) %collective-permute-start.1) | collective-permute-done | bytes 262176 | tf_op jit(solution)/shard_map/ppermute | solution.py:35
  14.9 0.0 collective-permute-start.2
  14.9 7.0 %collective-permute-done.2 = bf16[2,16,4096]{2,1,0:T(8,128)(2,1)S(1)} collective-permute-done((bf16[2,16,4096]{2,1,0:T(8,128)(2,1)S(1)}, bf16[2,16,4096]{2,1,0:T(8,128)(2,1)S(1)}, u32[]{:S(2)}, u32[]{:S(2)}) %collective-permute-start.2) | collective-permute-done | bytes 262176 | tf_op jit(solution)/shard_map/ppermute | solution.py:35
  21.9 0.0 collective-permute-start.3
  21.9 7.0 %collective-permute-done.3 = bf16[2,16,4096]{2,1,0:T(8,128)(2,1)S(1)} collective-permute-done((bf16[2,16,4096]{2,1,0:T(8,128)(2,1)S(1)}, bf16[2,16,4096]{2,1,0:T(8,128)(2,1)S(1)}, u32[]{:S(2)}, u32[]{:S(2)}) %collective-permute-start.3) | collective-permute-done | bytes 262176 | tf_op jit(solution)/shard_map/ppermute | solution.py:35
  28.9 0.0 collective-permute-start.4
  28.9 0.8 slice_bitcast_fusion.1
  29.7 6.2 %collective-permute-done.4 = bf16[2,16,4096]{2,1,0:T(8,128)(2,1)S(1)} collective-permute-done((bf16[2,16,4096]{2,1,0:T(8,128)(2,1)S(1)}, bf16[2,16,4096]{2,1,0:T(8,128)(2,1)S(1)}, u32[]{:S(2)}, u32[]{:S(2)}) %collective-permute-start.4) | collective-permute-done | bytes 262176 | tf_op jit(solution)/shard_map/ppermute | solution.py:35
  35.9 0.0 collective-permute-start.5
  35.9 0.1 pad_add_fusion
  36.0 0.9 convolution_bitcast_fusion
  36.9 6.1 %collective-permute-done.5 = bf16[2,16,4096]{2,1,0:T(8,128)(2,1)S(1)} collective-permute-done((bf16[2,16,4096]{2,1,0:T(8,128)(2,1)S(1)}, bf16[2,16,4096]{2,1,0:T(8,128)(2,1)S(1)}, u32[]{:S(2)}, u32[]{:S(2)}) %collective-permute-start.5) | collective-permute-done | bytes 262176 | tf_op jit(solution)/shard_map/ppermute | solution.py:35
  42.9 0.0 collective-permute-start.6
  42.9 0.1 slice_multiply_fusion
  43.0 0.1 broadcast_in_dim.28
  43.1 6.8 %collective-permute-done.6 = bf16[2,16,4096]{2,1,0:T(8,128)(2,1)S(1)} collective-permute-done((bf16[2,16,4096]{2,1,0:T(8,128)(2,1)S(1)}, bf16[2,16,4096]{2,1,0:T(8,128)(2,1)S(1)}, u32[]{:S(2)}, u32[]{:S(2)}) %collective-permute-start.6) | collective-permute-done | bytes 262176 | tf_op jit(solution)/shard_map/ppermute | solution.py:35
  50.1 1.0 constant_dynamic-update-slice_fusion.8
  51.1 0.0 slice-start
  51.3 0.0 copy-done
  51.3 0.5 fusion.3
  51.8 0.0 slice-start.1
  51.8 0.5 fusion.2
  52.3 0.4 add_convert_fusion
  52.8 0.5 slice-done
  53.3 1.5 slice-done.1
  54.8 1.3 fusion.1
  56.1 0.3 copy.12
  56.4 36.0 %all_to_all.33 = bf16[2,64,1024]{2,0,1:T(2,128)(2,1)S(1)} all-to-all(bf16[2,64,1024]{2,0,1:T(2,128)(2,1)S(1)} %copy.12), channel_id=1, replica_groups=mesh['day'=64,'pair'=8] {'day'}, dimensions={1} | all-to-all | bytes 524288 | tf_op jit(solution)/shard_map/all_to_all | solution.py:56
  92.4 0.2 convert_reduce_fusion
  92.6 0.6 broadcast_multiply_fusion
  94.0 0.2 fusion.20
  94.2 0.2 fusion.11
  94.4 0.1 fusion.9
  94.5 0.5 broadcast.37
  95.0 0.8 reduce.6
  95.8 0.8 reshape.58
  96.6 5.7 %all-to-all-start.1 = ((bf16[64,2,1024]{2,1,0:T(2,128)(2,1)}), bf16[64,2,1024]{2,1,0:T(2,128)(2,1)S(1)}, u32[]{:S(2)}, u32[]{:S(2)}) async-start(bf16[64,2,1024]{2,1,0:T(2,128)(2,1)} %reshape.58), calls=%async_computation.1 | async-start | bytes 524288 | tf_op jit(solution)/shard_map/all_to_all | solution.py:68
  102.4 82.9 %all-gather = f32[64,1,1024]{2,1,0:T(1,128)S(1)} all-gather(f32[1,1,1024]{2,1,0:T(1,128)S(1)} %fusion.15), channel_id=1, replica_groups=mesh['day'=64,'pair'=8] {'day'}, dimensions={0}, use_global_device_ids=true | all-gather | bytes 266240 | tf_op jit(solution)/shard_map/all_gather | solution.py:71
  185.3 0.8 copy.19
  186.0 0.0 all-to-all-done.1
  186.0 0.2 reshape.59
  186.3 1.5 reduce.4
  187.8 0.1 all_to_all.28
  187.9 0.8 copy.15
  (21 shorter events, 0.4 us)
Async XLA Ops:
  0.6 50.7 %copy-start = (bf16[2,16,4096]{2,1,0:T(8,128)(2,1)S(1)}, bf16[2,16,4096]{2,1,0:T(8,128)(2,1)}, u32[]{:S(2)}) copy-start(bf16[2,16,4096]{2,1,0:T(8,128)(2,1)} %param.5) | copy-start | bytes 786436
  0.6 7.2 %collective-permute-start = (bf16[2,16,4096]{2,1,0:T(8,128)(2,1)}, bf16[2,16,4096]{2,1,0:T(8,128)(2,1)S(1)}, u32[]{:S(2)}, u32[]{:S(2)}) collective-permute-start(bf16[2,16,4096]{2,1,0:T(8,128)(2,1)} %param.5), channel_id=1, source_target_pairs={{0,1},{1,2},{2,3},{3,4},{4,5},{5,6},{6,7},{7,0},{8,9},{9,10},{10,1... | collective-permute-start | bytes 786440 | tf_op jit(solution)/shard_map/ppermute | solution.py:35
  7.9 7.0 %collective-permute-start.1 = (bf16[2,16,4096]{2,1,0:T(8,128)(2,1)S(1)}, bf16[2,16,4096]{2,1,0:T(8,128)(2,1)S(1)}, u32[]{:S(2)}, u32[]{:S(2)}) collective-permute-start(bf16[2,16,4096]{2,1,0:T(8,128)(2,1)S(1)} %collective-permute-done), channel_id=1, source_target_pairs={{0,1},{1,2},{2,3},{3,4},{4,5},{5,6},{6,7},{7,0},{8,9},{9,10},{10,1... | collective-permute-start | bytes 786440 | tf_op jit(solution)/shard_map/ppermute | solution.py:35
  14.9 7.0 %collective-permute-start.2 = (bf16[2,16,4096]{2,1,0:T(8,128)(2,1)S(1)}, bf16[2,16,4096]{2,1,0:T(8,128)(2,1)S(1)}, u32[]{:S(2)}, u32[]{:S(2)}) collective-permute-start(bf16[2,16,4096]{2,1,0:T(8,128)(2,1)S(1)} %collective-permute-done.1), channel_id=1, source_target_pairs={{0,1},{1,2},{2,3},{3,4},{4,5},{5,6},{6,7},{7,0},{8,9},{9,10},{10,1... | collective-permute-start | bytes 786440 | tf_op jit(solution)/shard_map/ppermute | solution.py:35
  21.9 7.0 %collective-permute-start.3 = (bf16[2,16,4096]{2,1,0:T(8,128)(2,1)S(1)}, bf16[2,16,4096]{2,1,0:T(8,128)(2,1)S(1)}, u32[]{:S(2)}, u32[]{:S(2)}) collective-permute-start(bf16[2,16,4096]{2,1,0:T(8,128)(2,1)S(1)} %collective-permute-done.2), channel_id=1, source_target_pairs={{0,1},{1,2},{2,3},{3,4},{4,5},{5,6},{6,7},{7,0},{8,9},{9,10},{10,1... | collective-permute-start | bytes 786440 | tf_op jit(solution)/shard_map/ppermute | solution.py:35
  28.9 7.0 %collective-permute-start.4 = (bf16[2,16,4096]{2,1,0:T(8,128)(2,1)S(1)}, bf16[2,16,4096]{2,1,0:T(8,128)(2,1)S(1)}, u32[]{:S(2)}, u32[]{:S(2)}) collective-permute-start(bf16[2,16,4096]{2,1,0:T(8,128)(2,1)S(1)} %collective-permute-done.3), channel_id=1, source_target_pairs={{0,1},{1,2},{2,3},{3,4},{4,5},{5,6},{6,7},{7,0},{8,9},{9,10},{10,1... | collective-permute-start | bytes 786440 | tf_op jit(solution)/shard_map/ppermute | solution.py:35
  35.9 7.0 %collective-permute-start.5 = (bf16[2,16,4096]{2,1,0:T(8,128)(2,1)S(1)}, bf16[2,16,4096]{2,1,0:T(8,128)(2,1)S(1)}, u32[]{:S(2)}, u32[]{:S(2)}) collective-permute-start(bf16[2,16,4096]{2,1,0:T(8,128)(2,1)S(1)} %collective-permute-done.4), channel_id=1, source_target_pairs={{0,1},{1,2},{2,3},{3,4},{4,5},{5,6},{6,7},{7,0},{8,9},{9,10},{10,1... | collective-permute-start | bytes 786440 | tf_op jit(solution)/shard_map/ppermute | solution.py:35
  42.9 7.0 %collective-permute-start.6 = (bf16[2,16,4096]{2,1,0:T(8,128)(2,1)S(1)}, bf16[2,16,4096]{2,1,0:T(8,128)(2,1)S(1)}, u32[]{:S(2)}, u32[]{:S(2)}) collective-permute-start(bf16[2,16,4096]{2,1,0:T(8,128)(2,1)S(1)} %collective-permute-done.5), channel_id=1, source_target_pairs={{0,1},{1,2},{2,3},{3,4},{4,5},{5,6},{6,7},{7,0},{8,9},{9,10},{10,1... | collective-permute-start | bytes 786440 | tf_op jit(solution)/shard_map/ppermute | solution.py:35
  51.1 2.2 %slice-start = ((s8[8388608]{0:T(1024)(128)(4,1)}), s8[4194304]{0:T(1024)(128)(4,1)S(1)}, s32[]{:S(2)}) async-start(s8[8388608]{0:T(1024)(128)(4,1)} %bitcast.35), calls=%async_computation.2 | async-start | bytes 8388608
  51.8 2.9 %slice-start.1 = ((s8[8388608]{0:T(1024)(128)(4,1)}), s8[4194304]{0:T(1024)(128)(4,1)S(1)}, s32[]{:S(2)}) async-start(s8[8388608]{0:T(1024)(128)(4,1)} %bitcast.35), calls=%async_computation.3 | async-start | bytes 8388608
  54.8 39.2 %copy-start.1 = (bf16[128,128]{1,0:T(8,128)(2,1)S(1)}, bf16[128,128]{1,0:T(8,128)(2,1)}, u32[]{:S(2)}) copy-start(bf16[128,128]{1,0:T(8,128)(2,1)} %constant.55) | copy-start | bytes 98308
  96.6 89.4 %all-to-all-start.1 = ((bf16[64,2,1024]{2,1,0:T(2,128)(2,1)}), bf16[64,2,1024]{2,1,0:T(2,128)(2,1)S(1)}, u32[]{:S(2)}, u32[]{:S(2)}) async-start(bf16[64,2,1024]{2,1,0:T(2,128)(2,1)} %reshape.58), calls=%async_computation.1 | async-start | bytes 524288 | tf_op jit(solution)/shard_map/all_to_all | solution.py:68
